TPU v7x, 32 devices: a whole 2x2x4 slice. The times are simulated.
32 devices in a mesh: batch: 2 (over x), gx: 4 (over y, core), gy: 4 (over z).
Axes of the slice: x: 2, y: 2, z: 4, core: 2. Of those that a mesh axis runs over, the one named last changes fastest.
Arguments:
- features: bfloat16 [128, 64, 4, 256], P(('batch', 'gx'), 'gy'), parts along dimension 0, may hold values from -6 to 6
- conv_weight: bfloat16 [6912, 256], replicated, may hold values from -0.078125 to 0.078125
- down_weight: bfloat16 [2048, 512], replicated, may hold values from -0.125 to 0.125
- norm_gain: float32 [512], replicated, may hold values from 0.1 to 1.9
- qkv_weight: bfloat16 [512, 1536], replicated, may hold values from -0.25 to 0.25
- out_weight: bfloat16 [512, 512], replicated, may hold values from -0.25 to 0.25
- upstream: bfloat16 [64, 32, 2, 512], P(('batch', 'gx'), 'gy'), parts along dimension 0, may hold values from -6 to 6
Outputs:
- grad_features: bfloat16 [128, 64, 4, 256], P(('batch', 'gx'), 'gy'), parts along dimension 0
- grad_conv: bfloat16 [13824, 256], P(('batch', 'gx', 'gy')), parts along dimension 0
- grad_down: bfloat16 [4096, 512], P(('batch', 'gx', 'gy')), parts along dimension 0
- grad_gain: float32 [1024], P(('batch', 'gx', 'gy')), parts along dimension 0
- grad_qkv: bfloat16 [1024, 1536], P(('batch', 'gx', 'gy')), parts along dimension 0
- grad_out: bfloat16 [1024, 512], P(('batch', 'gx', 'gy')), parts along dimension 0
There are 2 independent parts, one for each index of `batch`. A program takes and returns all parts, laid end to end along the dimension named above; an argument that names none is the same for every part. Nothing has to cross between parts.
All inputs are finite; a program needn't handle non-finite values.
Results may differ from a plain program's by a relative error of at most 0.02.
Values may be sent and summed in bfloat16 or wider, within the bound.
A program may use at most 128 MiB of HBM per device.

v0:
```python
import jax
import jax.numpy as jnp
from jax import lax
from jax.sharding import PartitionSpec as P

H = 8
HD = 64


precise = lax.Precision.HIGHEST


def padded_2(block, sides, width):
    for axis, dim in sides:
        count = lax.axis_size(axis)
        forward = [(i, i + 1) for i in range(count - 1)]
        backward = [(target, source) for source, target in forward]
        low = lax.ppermute(
            lax.slice_in_dim(block, block.shape[dim] - width, None, axis=dim), axis, forward
        )
        high = lax.ppermute(lax.slice_in_dim(block, 0, width, axis=dim), axis, backward)
        block = jnp.concatenate([low, block, high], axis=dim)
    return block


def to_tokens(volume):
    extent_x, extent_y, extent_z, channels = volume.shape
    grid = volume.reshape(extent_x // 2, 2, extent_y // 2, 2, extent_z // 2, 2, channels)
    grid = grid.transpose(0, 2, 4, 1, 3, 5, 6)
    return grid.reshape(extent_x * extent_y * extent_z // 8, 8 * channels)


def from_tokens(matrix, extent_x, extent_y, extent_z):
    channels = matrix.shape[1] // 8
    grid = matrix.reshape(extent_x // 2, extent_y // 2, extent_z // 2, 2, 2, 2, channels)
    grid = grid.transpose(0, 3, 1, 4, 2, 5, 6)
    return grid.reshape(extent_x, extent_y, extent_z, channels)


def gather_patches(padded, extent_x, extent_y, extent_z, flipped):
    channels = padded.shape[3]
    pieces = []
    for offset_x in range(3):
        for offset_y in range(3):
            for offset_z in range(3):
                start_x = 2 - offset_x if flipped else offset_x
                start_y = 2 - offset_y if flipped else offset_y
                start_z = 2 - offset_z if flipped else offset_z
                pieces.append(
                    padded[
                        start_x : start_x + extent_x,
                        start_y : start_y + extent_y,
                        start_z : start_z + extent_z,
                    ]
                )
    joined = jnp.concatenate(pieces, axis=3)
    return joined.reshape(extent_x * extent_y * extent_z, 27 * channels)


def local(features, conv_weight, down_weight, norm_gain, qkv_weight, out_weight, upstream):
    extent_x, extent_y, extent_z, channels = features.shape
    model_width = out_weight.shape[0]
    voxels = extent_x * extent_y * extent_z
    score_scale = HD ** (-0.5)
    padded = padded_2(features, (("gx", 0), ("gy", 1)), 1)
    padded = jnp.pad(padded, ((0, 0), (0, 0), (1, 1), (0, 0)))
    patches = gather_patches(padded, extent_x, extent_y, extent_z, False)
    hidden = jnp.dot(patches, conv_weight, preferred_element_type=jnp.float32)
    gate_sig = jax.nn.sigmoid(hidden)
    activation = (hidden * gate_sig).astype(jnp.bfloat16)
    tokens_in = to_tokens(activation.reshape(extent_x, extent_y, extent_z, channels))
    tok_count = tokens_in.shape[0]
    trunk_rows = jnp.dot(tokens_in, down_weight, preferred_element_type=jnp.float32)
    mean_rows = jnp.mean(trunk_rows, axis=-1, keepdims=True)
    centred = trunk_rows - mean_rows
    inverse_std = lax.rsqrt(jnp.mean(centred * centred, axis=-1, keepdims=True) + 1e-05)
    normed = centred * inverse_std
    normed_b = (normed * norm_gain).astype(jnp.bfloat16)
    qkv_rows = jnp.dot(normed_b, qkv_weight, preferred_element_type=jnp.float32).astype(
        jnp.bfloat16
    )
    queries = qkv_rows[:, :model_width]
    local_keys = qkv_rows[:, model_width : 2 * model_width]
    local_values = qkv_rows[:, 2 * model_width :]
    all_keys, all_values = (
        lax.all_gather(local_keys, ("gx", "gy"), axis=0, tiled=True),
        lax.all_gather(local_values, ("gx", "gy"), axis=0, tiled=True),
    )
    queries_h = queries.reshape(tok_count, H, HD)
    keys_h = all_keys.reshape(-1, H, HD)
    values_h = all_values.reshape(-1, H, HD)
    scores = (
        jnp.einsum("ihe,jhe->hij", queries_h, keys_h, preferred_element_type=jnp.float32)
        * score_scale
    )
    exp_scores = jnp.exp(scores)
    totals = jnp.sum(exp_scores, axis=-1)
    attn_probs = exp_scores / totals[:, :, None]
    probs_b = attn_probs.astype(jnp.bfloat16)
    attended = jnp.einsum("hij,jhe->ihe", probs_b, values_h, preferred_element_type=jnp.float32)
    attended = attended.reshape(tok_count, model_width).astype(jnp.bfloat16)
    cotangent = upstream.reshape(tok_count, model_width)
    cot_float = cotangent.astype(jnp.float32)
    out_part = jnp.einsum("td,te->de", attended, cotangent, preferred_element_type=jnp.float32)
    d_attended = jnp.dot(cotangent, out_weight.T, preferred_element_type=jnp.float32).astype(
        jnp.bfloat16
    )
    d_att_h = d_attended.reshape(tok_count, H, HD)
    d_probs = jnp.einsum("ihe,jhe->hij", d_att_h, values_h, preferred_element_type=jnp.float32)
    d_probs = d_probs.astype(jnp.bfloat16).astype(jnp.float32)
    row_delta = jnp.sum(attn_probs * d_probs, axis=-1)
    d_scores = attn_probs * (d_probs - row_delta[:, :, None])
    d_queries = (
        jnp.einsum(
            "hij,jhe->ihe", d_scores, keys_h, precision=precise, preferred_element_type=jnp.float32
        )
        * score_scale
    )
    key_term = (
        jnp.einsum(
            "hij,ihe->jhe",
            d_scores,
            queries_h,
            precision=precise,
            preferred_element_type=jnp.float32,
        )
        * score_scale
    )
    value_term = jnp.einsum("hij,ihe->jhe", probs_b, d_att_h, preferred_element_type=jnp.float32)
    key_sums = lax.psum_scatter(
        jnp.concatenate(
            [
                key_term.reshape(tok_count * lax.axis_size(("gx", "gy")), model_width),
                value_term.reshape(tok_count * lax.axis_size(("gx", "gy")), model_width),
            ],
            axis=1,
        ).astype(jnp.bfloat16),
        ("gx", "gy"),
        scatter_dimension=0,
        tiled=True,
    ).astype(jnp.float32)
    d_keys = key_sums[:, :model_width].astype(jnp.bfloat16)
    d_values = key_sums[:, model_width:].astype(jnp.bfloat16)
    d_qkv = jnp.concatenate(
        [d_queries.reshape(tok_count, model_width).astype(jnp.bfloat16), d_keys, d_values], axis=1
    )
    qkv_part = jnp.einsum("td,te->de", normed_b, d_qkv, preferred_element_type=jnp.float32)
    d_normed = (
        jnp.dot(d_qkv, qkv_weight.T, preferred_element_type=jnp.float32)
        .astype(jnp.bfloat16)
        .astype(jnp.float32)
    )
    d_hat = d_normed * norm_gain
    gain_part = jnp.sum(d_normed * normed, axis=0)
    gain_sum = lax.psum_scatter(gain_part, ("gx", "gy"), scatter_dimension=0, tiled=True)
    d_trunk = cot_float + inverse_std * (
        d_hat
        - jnp.mean(d_hat, axis=-1, keepdims=True)
        - normed * jnp.mean(d_hat * normed, axis=-1, keepdims=True)
    )
    down_part = jnp.einsum(
        "tr,td->rd", tokens_in, d_trunk, precision=precise, preferred_element_type=jnp.float32
    )
    d_activation = jnp.dot(
        d_trunk, down_weight.T, precision=precise, preferred_element_type=jnp.float32
    ).astype(jnp.bfloat16)
    d_act_grid = (
        from_tokens(d_activation, extent_x, extent_y, extent_z)
        .reshape(voxels, channels)
        .astype(jnp.float32)
    )
    d_hidden = (d_act_grid * gate_sig * (1.0 + hidden * (1.0 - gate_sig))).astype(jnp.bfloat16)
    conv_part = jnp.einsum("vr,vc->rc", patches, d_hidden, preferred_element_type=jnp.float32)
    d_padded = padded_2(
        d_hidden.reshape(extent_x, extent_y, extent_z, channels), (("gx", 0), ("gy", 1)), 1
    )
    d_padded = jnp.pad(d_padded, ((0, 0), (0, 0), (1, 1), (0, 0)))
    d_patches = gather_patches(d_padded, extent_x, extent_y, extent_z, True)
    conv_flip = (
        conv_weight.reshape(27, channels, channels)
        .transpose(0, 2, 1)
        .reshape(27 * channels, channels)
    )
    grad_features = jnp.dot(d_patches, conv_flip, preferred_element_type=jnp.float32)
    grad_features = grad_features.reshape(extent_x, extent_y, extent_z, channels).astype(
        jnp.bfloat16
    )
    conv_sum, down_sum, qkv_sum, out_sum = (
        lax.psum_scatter(
            conv_part.astype(jnp.bfloat16), ("gx", "gy"), scatter_dimension=0, tiled=True
        ).astype(jnp.float32),
        lax.psum_scatter(
            down_part.astype(jnp.bfloat16), ("gx", "gy"), scatter_dimension=0, tiled=True
        ).astype(jnp.float32),
        lax.psum_scatter(
            qkv_part.astype(jnp.bfloat16), ("gx", "gy"), scatter_dimension=0, tiled=True
        ).astype(jnp.float32),
        lax.psum_scatter(
            out_part.astype(jnp.bfloat16), ("gx", "gy"), scatter_dimension=0, tiled=True
        ).astype(jnp.float32),
    )
    return (
        grad_features,
        conv_sum.astype(jnp.bfloat16),
        down_sum.astype(jnp.bfloat16),
        gain_sum,
        qkv_sum.astype(jnp.bfloat16),
        out_sum.astype(jnp.bfloat16),
    )


def solution(mesh):
    placed = (
        P(("batch", "gx"), "gy", None, None),
        P(),
        P(),
        P(),
        P(),
        P(),
        P(("batch", "gx"), "gy", None, None),
    )
    return jax.shard_map(
        local,
        mesh=mesh,
        in_specs=placed,
        out_specs=(
            P(("batch", "gx"), "gy", None, None),
            P(("batch", "gx", "gy"), None),
            P(("batch", "gx", "gy"), None),
            P(("batch", "gx", "gy")),
            P(("batch", "gx", "gy"), None),
            P(("batch", "gx", "gy"), None),
        ),
        check_vma=False,
    )
```

profile of v0, /device:TPU:0, one launch (start us, length us, event | category | flops | bytes accessed | tf_op | source)
XLA Modules:
  0.0 543.9 jit_solution(16023638373138928668)
XLA Ops:
  15.8 3.5 collective-permute-start.2
  20.9 4.2 collective-permute-done.3
  57.6 22.5 %reshape.89 = bf16[1024,6912]{1,0:T(8,128)(2,1)} reshape(bf16[16,16,4,6912]{3,2,1,0:T(4,128)(2,1)} %slice_dynamic-update-slice_fusion.18) | data formatting | bytes 28311552 | tf_op jit(solution)/shard_map/reshape | solution.py:57
  80.1 10.9 %multiply_convert_fusion.2 = (bf16[1024,256]{1,0:T(8,128)(2,1)S(1)}, f32[1024,256]{1,0:T(8,128)}) fusion(bf16[1024,6912]{1,0:T(8,128)(2,1)} %reshape.89, bf16[6912,256]{1,0:T(8,128)(2,1)} %param.8), kind=kOutput, calls=%fused_computation.54 | convolution fusion | flops 3625189376 | bytes 19267584 | tf_op jit(solution)/shard_map/dot_general | solution.py:68
  98.7 39.4 %all-gather.3.cloned.1.call-done = bf16[2048,512]{1,0:T(8,128)(2,1)} async-done(((bf16[128,512]{1,0:T(8,128)(2,1)}), bf16[2048,512]{1,0:T(8,128)(2,1)}) %all-gather.3.cloned.1.call-update) | async-done | bytes 2097168 | tf_op jit(solution)/shard_map/all_gather | solution.py:86
  138.1 4.5 copy.45
  145.7 3.3 copy-done.2
  151.9 29.2 %all-gather.5.cloned.1.call-done = bf16[2048,512]{1,0:T(8,128)(2,1)} async-done(((bf16[128,512]{1,0:T(8,128)(2,1)}), bf16[2048,512]{1,0:T(8,128)(2,1)}) %all-gather.5.cloned.1.call-update) | async-done | bytes 2097168 | tf_op jit(solution)/shard_map/all_gather | solution.py:87
  181.1 4.0 copy.48
  185.1 6.7 %fusion = (f32[8,128]{1,0:T(8,128)S(1)}, bf16[8,128,2048]{2,1,0:T(8,128)(2,1)S(1)}) fusion(f32[8,128]{1,0:T(8,128)S(1)} %get-tuple-element.44, f32[8,128,2048]{2,1,0:T(8,128)} %copy-done.2, bf16[128,8,64]{0,2,1:T(8,128)(2,1)S(1)} %bitcast.71, bf16[2048,8,64]{0,2,1:T(8,128)(2,1)} %bitcast.61), kind=kOutput, calls=%fused_computation.3 | convolution fusion | flops 281017344 | bytes 14819328 | tf_op jit(solution)/shard_map/ihe,jhe->hij/dot_general | solution.py:109
  191.8 5.9 %multiply_convert_fusion = bf16[8,64,2048]{2,1,0:T(8,128)(2,1)S(1)} fusion(bf16[128,8,64]{0,2,1:T(8,128)(2,1)S(1)} %bitcast.67, bf16[8,128,2048]{2,1,0:T(8,128)(2,1)S(1)} %get-tuple-element.47, f32[8,128]{1,0:T(8,128)S(1)} %get-tuple-element.46, f32[8,128,2048]{2,1,0:T(8,128)S(1)} %copy-done.3, f32[8,128]{1,0:T(8,128)S(1)} %get-tuple-element.44), kind=kOutput, calls=%fused_computation.11 | convolution fusion | flops 1623195648 | bytes 14819328 | tf_op jit(solution)/shard_map/hij,ihe->jhe/dot_general | solution.py:120
  200.3 6.4 %copy.59 = bf16[2048,1024]{1,0:T(8,128)(2,1)} copy(bf16[2048,1024]{0,1:T(8,128)(2,1)} %pad_maximum_fusion) | data formatting | bytes 8388608
  206.7 5.7 %fusion.31 = bf16[8,64,128]{2,1,0:T(8,128)(2,1)S(1)} fusion(bf16[2048,8,64]{0,2,1:T(8,128)(2,1)} %bitcast.62, f32[8,128,2048]{2,1,0:T(8,128)} %copy-done.2, f32[8,128]{1,0:T(8,128)S(1)} %get-tuple-element.44), kind=kOutput, calls=%fused_computation.47 | convolution fusion | flops 274792448 | bytes 10620928 | tf_op jit(solution)/shard_map/hij,jhe->ihe/dot_general | solution.py:100
  213.8 12.6 %fusion.34 = bf16[8,64,128]{2,1,0:T(8,128)(2,1)S(1)} fusion(bf16[2048,8,64]{0,2,1:T(8,128)(2,1)} %bitcast.57, bf16[8,128,2048]{2,1,0:T(8,128)(2,1)} %copy-done.14, f32[8,128]{1,0:T(8,128)S(1)} %get-tuple-element.46, f32[8,128,2048]{2,1,0:T(8,128)} %copy-done.2, f32[8,128]{1,0:T(8,128)S(1)} %get-tuple-element.44), kind=kOutput, calls=%fused_computation.49 | convolution fusion | flops 1621229568 | bytes 14819328 | tf_op jit(solution)/shard_map/hij,jhe->ihe/dot_general | solution.py:114
  226.4 51.7 %reduce-scatter.16.cloned.1.call-done = bf16[128,1024]{1,0:T(8,128)(2,1)} async-done(((bf16[2048,1024]{1,0:T(8,128)(2,1)}), bf16[128,1024]{1,0:T(8,128)(2,1)}) %reduce-scatter.16.cloned.1.call-update) | async-done | bytes 262160
  284.0 3.3 convolution_convert_fusion.2
  301.0 5.7 %copy.56 = bf16[27,256,256]{2,1,0:T(8,128)(2,1)} copy(bf16[27,256,256]{1,2,0:T(8,128)(2,1)} %bitcast.59) | data formatting | bytes 7077888 | tf_op jit(solution)/shard_map/transpose | solution.py:181
  314.8 3.6 collective-permute-start.6
  319.7 10.7 %convolution_convert_fusion = bf16[6912,256]{1,0:T(8,128)(2,1)} fusion(bf16[1024,6912]{1,0:T(8,128)(2,1)} %reshape.89, bf16[1024,256]{1,0:T(8,128)(2,1)} %copy-done.6), kind=kOutput, calls=%fused_computation.2 | convolution fusion | flops 3625648128 | bytes 18219008 | tf_op jit(solution)/shard_map/vr,vc->rc/dot_general | solution.py:173
  330.5 32.6 %all-reduce.2 = f32[512]{0:T(512)S(1)} all-reduce(f32[512]{0:T(512)S(1)} %copy-done.12), channel_id=5, replica_groups=mesh['batch'=2,'gx'=4,'gy'=4] {'gx','gy'}, use_global_device_ids=true, to_apply=%region_10.11.clone | all-reduce | flops 512 | bytes 4096
  369.0 3.8 convolution_convert_fusion.7
  373.9 26.1 %reduce-scatter.12.cloned.1.call-done = bf16[32,1536]{1,0:T(8,128)(2,1)} async-done(((bf16[512,1536]{1,0:T(8,128)(2,1)}), bf16[32,1536]{1,0:T(8,128)(2,1)}) %reduce-scatter.12.cloned.1.call-update) | async-done | bytes 98320 | tf_op jit(solution)/shard_map/reduce_scatter | solution.py:195
  400.0 65.3 %reduce-scatter.10.cloned.1.call-done = bf16[128,512]{1,0:T(8,128)(2,1)} async-done(((bf16[2048,512]{1,0:T(8,128)(2,1)}), bf16[128,512]{1,0:T(8,128)(2,1)}) %reduce-scatter.10.cloned.1.call-update) | async-done | bytes 131088 | tf_op jit(solution)/shard_map/reduce_scatter | solution.py:192
  465.2 71.5 %reduce-scatter.8.cloned.1.call-done = bf16[432,256]{1,0:T(8,128)(2,1)} async-done(((bf16[6912,256]{1,0:T(8,128)(2,1)}), bf16[432,256]{1,0:T(8,128)(2,1)}) %reduce-scatter.8.cloned.1.call-update) | async-done | bytes 221200 | tf_op jit(solution)/shard_map/reduce_scatter | solution.py:189
  (157 shorter events, 95.1 us)
Async XLA Ops:
  7.2 84.8 %copy-start = (bf16[2048,512]{1,0:T(8,128)(2,1)S(1)}, bf16[2048,512]{1,0:T(8,128)(2,1)}, u32[]{:S(2)}) copy-start(bf16[2048,512]{1,0:T(8,128)(2,1)} %param.9) | copy-start | bytes 6291460
  7.2 130.9 %all-gather.3.cloned.1.call-start = ((), (), s32[]{:S(2)}) async-start(), calls=%async_computation.5 | async-start | bytes 2228224 | tf_op jit(solution)/shard_map/all_gather | solution.py:86
  8.2 3.7 collective-permute-start
  10.5 5.2 collective-permute-start.1
  11.9 29.7 %copy-start.1 = (bf16[16,16,4,256]{3,2,1,0:T(4,128)(2,1)S(1)}, bf16[16,16,4,256]{3,2,1,0:T(4,128)(2,1)}, u32[]{:S(2)}) copy-start(bf16[16,16,4,256]{3,2,1,0:T(4,128)(2,1)} %param.7) | copy-start | bytes 1572868
  15.8 5.1 collective-permute-start.2
  19.3 5.9 %collective-permute-start.3 = (bf16[18,1,4,256]{3,2,1,0:T(4,128)(2,1)S(1)}, bf16[18,1,4,256]{3,2,1,0:T(4,128)(2,1)S(1)}, u32[]{:S(2)}, u32[]{:S(2)}) collective-permute-start(bf16[18,1,4,256]{3,2,1,0:T(4,128)(2,1)S(1)} %get-tuple-element.30), channel_id=1, source_target_pairs={{1,0},{2,1},{3,2},{5,4},{6,5},{7,6},{9,8},{10,9},{11,10},{13,12},{... | collective-permute-start | bytes 110600 | tf_op jit(solution)/shard_map/ppermute | solution.py:21
  80.1 12.6 %copy-start.10 = (f32[512]{0:T(512)S(1)}, f32[512]{0:T(512)}, u32[]{:S(2)}) copy-start(f32[512]{0:T(512)} %param.10) | copy-start | bytes 6148
  95.3 85.8 %all-gather.5.cloned.1.call-start = ((), (), s32[]{:S(2)}) async-start(), calls=%async_computation.6 | async-start | bytes 2228224 | tf_op jit(solution)/shard_map/all_gather | solution.py:87
  96.1 182.1 %reduce-scatter.16.cloned.1.call-start = ((), (), s32[]{:S(2)}) async-start(), calls=%async_computation.11 | async-start | bytes 4456448
  185.1 6.8 %copy-start.3 = (f32[8,128,2048]{2,1,0:T(8,128)S(1)}, f32[8,128,2048]{2,1,0:T(8,128)}, u32[]{:S(2)}) copy-start(f32[8,128,2048]{2,1,0:T(8,128)} %copy-done.2) | copy-start | bytes 25165828
  191.8 5.9 %copy-start.14 = (bf16[8,128,2048]{2,1,0:T(8,128)(2,1)}, bf16[8,128,2048]{2,1,0:T(8,128)(2,1)S(1)}, u32[]{:S(2)}) copy-start(bf16[8,128,2048]{2,1,0:T(8,128)(2,1)S(1)} %get-tuple-element.47) | copy-start | bytes 12582916
  191.8 5.9 %copy-start.7 = (bf16[8,64,2048]{2,1,0:T(8,128)(2,1)S(1)}, bf16[8,64,2048]{2,1,0:T(8,128)(2,1)}, u32[]{:S(2)}) copy-start(bf16[8,64,2048]{2,1,0:T(8,128)(2,1)} %convolution_convert_fusion.4) | copy-start | bytes 6291460
  206.7 167.2 %reduce-scatter.14.cloned.1.call-start = ((), (), s32[]{:S(2)}) async-start(), calls=%async_computation.10 | async-start | bytes 557056 | tf_op jit(solution)/shard_map/reduce_scatter | solution.py:198
  213.6 186.4 %reduce-scatter.12.cloned.1.call-start = ((), (), s32[]{:S(2)}) async-start(), calls=%async_computation.9 | async-start | bytes 1671168 | tf_op jit(solution)/shard_map/reduce_scatter | solution.py:195
  226.4 54.7 %copy-start.9 = (bf16[8,64,128]{2,1,0:T(8,128)(2,1)}, bf16[8,64,128]{2,1,0:T(8,128)(2,1)S(1)}, u32[]{:S(2)}) copy-start(bf16[8,64,128]{2,1,0:T(8,128)(2,1)S(1)} %fusion.34) | copy-start | bytes 393220
  281.2 184.1 %reduce-scatter.10.cloned.1.call-start = ((), (), s32[]{:S(2)}) async-start(), calls=%async_computation.8 | async-start | bytes 2228224 | tf_op jit(solution)/shard_map/reduce_scatter | solution.py:192
  287.4 249.4 %reduce-scatter.8.cloned.1.call-start = ((), (), s32[]{:S(2)}) async-start(), calls=%async_computation.7 | async-start | bytes 3760128 | tf_op jit(solution)/shard_map/reduce_scatter | solution.py:189
  290.8 16.0 %copy-start.13 = (u32[32]{0:T(128)S(1)}, u32[32]{0:T(128)}, u32[]{:S(2)}) copy-start(u32[32]{0:T(128)} %constant.25) | copy-start | bytes 388
  299.7 11.6 %collective-permute-start.4 = (bf16[1,16,4,256]{3,1,2,0:T(8,128)(2,1)S(1)}, bf16[1,16,4,256]{3,1,2,0:T(8,128)(2,1)S(1)}, u32[]{:S(2)}, u32[]{:S(2)}) collective-permute-start(bf16[1,16,4,256]{3,1,2,0:T(8,128)(2,1)S(1)} %copy.50), channel_id=1, source_target_pairs={{0,4},{4,8},{8,12},{1,5},{5,9},{9,13},{2,6},{6,10},{10,14},{3,7},{... | collective-permute-start | bytes 98312 | tf_op jit(solution)/shard_map/ppermute | solution.py:18
  310.1 4.0 collective-permute-start.5
  314.8 48.9 %collective-permute-start.6 = (bf16[18,1,4,256]{3,1,2,0:T(2,128)(2,1)}, bf16[18,1,4,256]{3,1,2,0:T(2,128)(2,1)S(1)}, u32[]{:S(2)}, u32[]{:S(2)}) collective-permute-start(bf16[18,1,4,256]{3,1,2,0:T(2,128)(2,1)} %get-tuple-element.27), channel_id=1, source_target_pairs={{0,1},{1,2},{2,3},{4,5},{5,6},{6,7},{8,9},{9,10},{10,11},{12,13},{... | collective-permute-start | bytes 110600 | tf_op jit(solution)/shard_map/ppermute | solution.py:18
  318.4 12.1 %copy-start.12 = (f32[512]{0:T(512)S(1)}, f32[512]{0:T(512)}, u32[]{:S(2)}) copy-start(f32[512]{0:T(512)} %get-tuple-element.24) | copy-start | bytes 6148
  318.4 45.2 %collective-permute-start.7 = (bf16[18,1,4,256]{3,1,2,0:T(2,128)(2,1)S(1)}, bf16[18,1,4,256]{3,1,2,0:T(2,128)(2,1)S(1)}, u32[]{:S(2)}, u32[]{:S(2)}) collective-permute-start(bf16[18,1,4,256]{3,1,2,0:T(2,128)(2,1)S(1)} %get-tuple-element.28), channel_id=1, source_target_pairs={{1,0},{2,1},{3,2},{5,4},{6,5},{7,6},{9,8},{10,9},{11,10},{13,12},{... | collective-permute-start | bytes 110600 | tf_op jit(solution)/shard_map/ppermute | solution.py:21
  (6 other events, 17.1 us)
Sparse Core Ops, SparseCore 0:
  95.4 42.6 all-gather.2
  140.9 40.1 all-gather.4
  206.8 71.3 reduce-scatter.15
  282.6 54.7 reduce-scatter.13
  341.5 58.4 reduce-scatter.11
  404.6 60.6 reduce-scatter.9
  469.7 67.0 reduce-scatter.7
where the time goes:
time: 552 us; the launch traced here: 544 us
  waiting for transfers between devices  293 us (53%)
  local copies, waits for them, and re-layouts  90.6 us (16%)
  matrix products  78.3 us (14%)
  blocking collectives  32.6 us (6%)
  other arithmetic  17.6 us (3%)
  starting transfers between devices  16.6 us (3%)
  between operations  15.6 us (3%)
    reduce_scatter x1, waiting for transfers between devices, local(): lax.psum_scatter(conv_part.astype(jnp.bfloat16), ('gx', 'gy'), scatter_di...  71.5 us
    reduce_scatter x1, waiting for transfers between devices, local(): lax.psum_scatter(down_part.astype(jnp.bfloat16), ('gx', 'gy'), scatter_di...  65.3 us
    unnamed x8, waiting for transfers between devices  52.5 us
    all_gather x1, waiting for transfers between devices, local(): lax.all_gather(local_keys, ('gx', 'gy'), axis=0, tiled=True)  39.4 us
    unnamed x74, local copies, waits for them, and re-layouts  38.3 us
    unnamed x1, blocking collectives  32.6 us
    all_gather x1, waiting for transfers between devices, local(): lax.all_gather(local_values, ('gx', 'gy'), axis=0, tiled=True)  29.2 us
    reduce_scatter x1, waiting for transfers between devices, local(): lax.psum_scatter(qkv_part.astype(jnp.bfloat16), ('gx', 'gy'), scatter_dim...  26.1 us
  transfers between devices with their start and end apart: 15, of which 10 were waited for; matrix products, arithmetic and copies ran while one was open for 16% of the time, Pallas kernels for 0%

commit v1 on v0

v1 whole, which is shorter than its diff:
```python
import functools

import jax
import jax.numpy as jnp
from jax import lax
from jax.experimental import pallas as pl
from jax.experimental.pallas import tpu as pltpu
from jax.sharding import PartitionSpec as P

H = 8
HD = 64
MESH = pl.DeviceIdType.MESH
BF = jnp.bfloat16
F32 = jnp.float32


def halo(block, sides):
    for axis, dim in sides:
        count = lax.axis_size(axis)
        forward = [(i, i + 1) for i in range(count - 1)]
        backward = [(target, source) for source, target in forward]
        low = lax.ppermute(
            lax.slice_in_dim(block, block.shape[dim] - 1, None, axis=dim), axis, forward
        )
        high = lax.ppermute(lax.slice_in_dim(block, 0, 1, axis=dim), axis, backward)
        block = jnp.concatenate([low, block, high], axis=dim)
    return block


def patches_of(padded, z, x, y, flipped):
    shifted = [padded[:, :, o : o + y] for o in range(3)]
    pieces = []
    for ox in range(3):
        for oy in range(3):
            for oz in range(3):
                sx, sy, sz = (2 - ox, 2 - oy, 2 - oz) if flipped else (ox, oy, oz)
                pieces.append(shifted[sy][sz : sz + z, sx : sx + x])
    joined = jnp.concatenate(pieces, axis=3)
    return joined.reshape(z * x * y, joined.shape[3])


def to_tokens(cells, z, x, y):
    channels = cells.shape[-1]
    grid = cells.reshape(z // 2, 2, x // 2, 2, y // 2, 2, channels)
    grid = grid.transpose(2, 4, 0, 3, 5, 1, 6)
    return grid.reshape(z * x * y // 8, 8 * channels)


def from_tokens(matrix, z, x, y):
    channels = matrix.shape[1] // 8
    grid = matrix.reshape(x // 2, y // 2, z // 2, 2, 2, 2, channels)
    grid = grid.transpose(2, 5, 0, 3, 1, 4, 6)
    return grid.reshape(z * x * y, channels)


def peer_of(index, n_gy):
    return {"gx": index // n_gy, "gy": lax.rem(index, n_gy)}


def attention_kernel(
    n, n_gy, send_ref, dqo_ref, dkv_ref, recv, back, home, e_buf, dp_buf, acc, s1, r1, s2, r2
):
    rows = send_ref.shape[1]
    half = rows // 3
    me = lax.axis_index("gx") * n_gy + lax.axis_index("gy")
    barrier = pltpu.get_barrier_semaphore()

    def greet(i, carry):
        pl.semaphore_signal(
            barrier, inc=1, device_id=peer_of(lax.rem(me + i, n), n_gy), device_id_type=MESH
        )
        return carry

    lax.fori_loop(1, n, greet, 0)
    pl.semaphore_wait(barrier, n - 1)

    def send(src, dst, ssem, rsem):
        def body(i, carry):
            peer = lax.rem(me + i, n)
            pltpu.make_async_remote_copy(
                src_ref=src.at[peer],
                dst_ref=dst.at[me],
                send_sem=ssem.at[i],
                recv_sem=rsem.at[i],
                device_id=peer_of(peer, n_gy),
                device_id_type=MESH,
            ).start()
            return carry

        lax.fori_loop(1, n, body, 0)

    def finish(src, dst, ssem, rsem):
        def body(i, carry):
            peer = lax.rem(me + i, n)
            source = lax.rem(me + n - i, n)
            pltpu.make_async_remote_copy(
                src_ref=src.at[peer],
                dst_ref=dst.at[source],
                send_sem=ssem.at[i],
                recv_sem=rsem.at[i],
                device_id=peer_of(peer, n_gy),
                device_id_type=MESH,
            ).wait()
            return carry

        lax.fori_loop(1, n, body, 0)

    send(send_ref, recv, s1, r1)
    recv[pl.ds(me, 1)] = send_ref[pl.ds(me, 1)]
    finish(send_ref, recv, s1, r1)

    group = 256 // half
    kgroup = 256 // (2 * half)
    n_k = n // kgroup
    low = lax.broadcasted_iota(jnp.int32, (256, 128), 1) < HD
    acc[...] = jnp.zeros_like(acc)

    def keys_of(kc):
        return recv[kc * kgroup : (kc + 1) * kgroup, half:].reshape(256, 128)

    def block(b, carry):
        qd = recv[pl.ds(b * group, group), :half].reshape(256, 128)
        zero = jnp.zeros_like(qd)
        q0 = jnp.where(low, qd * BF(HD**-0.5), zero)
        d0 = jnp.where(low, zero, qd)
        nt = (((1,), (1,)), ((), ()))
        total = jnp.zeros((1, 256), F32)
        delta = jnp.zeros((1, 256), F32)
        for kc in range(n_k):
            kv = keys_of(kc)
            e = jnp.exp(lax.dot_general(kv, q0, nt, preferred_element_type=F32))
            dp = lax.dot_general(kv, d0, nt, preferred_element_type=F32)
            e_buf[kc] = e
            dp_buf[kc] = dp
            total = total + jnp.sum(e, axis=0, keepdims=True)
            delta = delta + jnp.sum(e * dp, axis=0, keepdims=True)
        inverse = 1.0 / total
        delta = delta * inverse
        qd0 = jnp.concatenate([q0, d0], axis=0)
        dq_t = jnp.zeros((128, 256), F32)
        o_t = jnp.zeros((128, 256), F32)
        for kc in range(n_k):
            p = e_buf[kc] * inverse
            ds = (p * (dp_buf[kc] - delta)).astype(BF)
            pb = p.astype(BF)
            kv_t = keys_of(kc).T
            dq_t = dq_t + jnp.dot(kv_t, ds, preferred_element_type=F32)
            o_t = o_t + jnp.dot(kv_t, pb, preferred_element_type=F32)
            acc[kc] += jnp.dot(
                jnp.concatenate([ds, pb], axis=1), qd0, preferred_element_type=F32
            )
        dqo_t = jnp.concatenate([dq_t[:HD] * HD**-0.5, o_t[HD:]], axis=0)
        back[pl.ds(b * group, group), :half] = dqo_t.T.astype(BF).reshape(group, half, 128)
        return carry

    lax.fori_loop(0, n // group, block, 0)
    for kc in range(n_k):
        back[kc * kgroup : (kc + 1) * kgroup, half:] = (
            acc[kc].astype(BF).reshape(kgroup, 2 * half, 128)
        )

    send(back, home, s2, r2)
    home[pl.ds(me, 1)] = back[pl.ds(me, 1)]
    finish(back, home, s2, r2)
    for h in range(H):
        dqo_ref[h] = home[2 * h : 2 * h + 2, :half].reshape(2 * half, 128)
        dkv_ref[h] = (home[2 * h, half:].astype(F32) + home[2 * h + 1, half:].astype(F32)).astype(
            BF
        )


def attention(send):
    n_gy = lax.axis_size("gy")
    n, rows, width = send.shape
    tokens = rows // 3 * 2
    vm = pl.BlockSpec(memory_space=pltpu.VMEM)
    n_k = n * tokens // 256
    return pl.pallas_call(
        functools.partial(attention_kernel, n, n_gy),
        out_shape=(
            jax.ShapeDtypeStruct((H, tokens, width), BF),
            jax.ShapeDtypeStruct((H, tokens, width), BF),
        ),
        in_specs=[vm],
        out_specs=(vm, vm),
        scratch_shapes=[
            pltpu.VMEM(send.shape, BF),
            pltpu.VMEM(send.shape, BF),
            pltpu.VMEM(send.shape, BF),
            pltpu.VMEM((n_k, 256, 256), F32),
            pltpu.VMEM((n_k, 256, 256), F32),
            pltpu.VMEM((n_k, 256, 128), F32),
            pltpu.SemaphoreType.DMA((n,)),
            pltpu.SemaphoreType.DMA((n,)),
            pltpu.SemaphoreType.DMA((n,)),
            pltpu.SemaphoreType.DMA((n,)),
        ],
        compiler_params=pltpu.CompilerParams(
            collective_id=0, has_side_effects=True, vmem_limit_bytes=40 * 1024 * 1024
        ),
        cost_estimate=pl.CostEstimate(
            flops=2_000_000_000, bytes_accessed=2_000_000, transcendentals=2_000_000
        ),
    )(send)


def local(features, conv_weight, down_weight, norm_gain, qkv_weight, out_weight, upstream):
    x, y, z, channels = features.shape
    width = out_weight.shape[0]
    group = lax.axis_size("gx") * lax.axis_size("gy")
    cells = features.transpose(2, 0, 1, 3)
    padded = halo(cells, (("gx", 1), ("gy", 2)))
    padded = jnp.pad(padded, ((1, 1), (0, 0), (0, 0), (0, 0)))
    patches = patches_of(padded, z, x, y, False)
    hidden = jnp.dot(patches, conv_weight, preferred_element_type=F32)
    gate_sig = jax.nn.sigmoid(hidden)
    activation = (hidden * gate_sig).astype(BF)
    tokens_in = to_tokens(activation, z, x, y)
    tokens = tokens_in.shape[0]
    trunk = jnp.dot(tokens_in, down_weight, preferred_element_type=F32)
    centred = trunk - jnp.mean(trunk, axis=-1, keepdims=True)
    inverse_std = lax.rsqrt(jnp.mean(centred * centred, axis=-1, keepdims=True) + 1e-05)
    normed = centred * inverse_std
    normed_b = (normed * norm_gain).astype(BF)
    cotangent = upstream.reshape(tokens, width)

    w_kv = (
        qkv_weight[:, width:].reshape(width, 2, H, HD).transpose(0, 2, 1, 3).reshape(width, -1)
    )
    w_q = qkv_weight[:, :width]
    kv = jnp.dot(normed_b, w_kv, preferred_element_type=F32).astype(BF)
    queries = jnp.dot(normed_b, w_q, preferred_element_type=F32).astype(BF)
    d_attended = lax.dot_general(
        cotangent, out_weight, (((1,), (1,)), ((), ())), preferred_element_type=F32
    ).astype(BF)
    qd = jnp.concatenate(
        [queries.reshape(tokens, H, HD), d_attended.reshape(tokens, H, HD)], axis=2
    )
    qd = qd.reshape(2, tokens // 2, H, 2 * HD).transpose(2, 0, 1, 3)
    kv_h = kv.reshape(tokens, H, 2 * HD).transpose(1, 0, 2)
    kv_h = jnp.broadcast_to(kv_h[:, None], (H, 2, tokens, 2 * HD))
    send = jnp.concatenate([qd, kv_h], axis=2).reshape(group, tokens * 3 // 2, 2 * HD)
    dqo, dkv = attention(send)
    dqo = dqo.transpose(1, 0, 2)
    attended = dqo[:, :, HD:].reshape(tokens, width)
    d_q = dqo[:, :, :HD].reshape(tokens, width)
    d_kv = dkv.transpose(1, 0, 2).reshape(tokens, 2 * width)
    d_qkv = jnp.concatenate([d_q, d_kv], axis=1)
    w_all = jnp.concatenate([w_q, w_kv], axis=1)

    tn = (((0,), (0,)), ((), ()))
    nt = (((1,), (1,)), ((), ()))
    out_part = lax.dot_general(attended, cotangent, tn, preferred_element_type=F32)
    qkv_part = lax.dot_general(normed_b, d_qkv, tn, preferred_element_type=F32)
    d_normed = lax.dot_general(d_qkv, w_all, nt, preferred_element_type=F32)
    d_hat = d_normed * norm_gain
    gain_part = jnp.sum(d_normed * normed, axis=0)
    d_trunk = cotangent.astype(F32) + inverse_std * (
        d_hat
        - jnp.mean(d_hat, axis=-1, keepdims=True)
        - normed * jnp.mean(d_hat * normed, axis=-1, keepdims=True)
    )
    d_trunk = d_trunk.astype(BF)
    down_part = lax.dot_general(tokens_in, d_trunk, tn, preferred_element_type=F32)
    d_activation = lax.dot_general(d_trunk, down_weight, nt, preferred_element_type=F32).astype(BF)
    d_act = from_tokens(d_activation, z, x, y).astype(F32)
    d_hidden = (d_act * gate_sig * (1.0 + hidden * (1.0 - gate_sig))).astype(BF)
    conv_part = lax.dot_general(patches, d_hidden, tn, preferred_element_type=F32)
    d_padded = halo(d_hidden.reshape(z, x, y, channels), (("gx", 1), ("gy", 2)))
    d_padded = jnp.pad(d_padded, ((1, 1), (0, 0), (0, 0), (0, 0)))
    d_patches = patches_of(d_padded, z, x, y, True)
    conv_flip = (
        conv_weight.reshape(27, channels, channels)
        .transpose(0, 2, 1)
        .reshape(27 * channels, channels)
    )
    grad_features = jnp.dot(d_patches, conv_flip, preferred_element_type=F32).astype(BF)
    grad_features = grad_features.reshape(z, x, y, channels).transpose(1, 2, 0, 3)
    conv_sum, down_sum, qkv_sum, out_sum, gain_sum = reduce_all(
        conv_part.astype(BF), down_part.astype(BF), qkv_part.astype(BF), out_part.astype(BF),
        gain_part,
    )
    kv_sum = qkv_sum[:, width:].reshape(-1, H, 2, HD).transpose(0, 2, 1, 3).reshape(-1, 2 * width)
    qkv_sum = jnp.concatenate([qkv_sum[:, :width], kv_sum], axis=1)
    return grad_features, conv_sum, down_sum, gain_sum, qkv_sum, out_sum


def reduce_all(conv_part, down_part, qkv_part, out_part, gain_part):
    def scatter(part):
        return lax.psum_scatter(part, ("gx", "gy"), scatter_dimension=0, tiled=True)

    gains = lax.all_gather(gain_part, ("gx", "gy"), axis=0)
    me = lax.axis_index(("gx", "gy"))
    size = gain_part.shape[0] // gains.shape[0]
    gain_sum = lax.dynamic_slice_in_dim(jnp.sum(gains, axis=0), me * size, size, 0)
    return scatter(conv_part), scatter(down_part), scatter(qkv_part), scatter(out_part), gain_sum


def solution(mesh):
    placed = (
        P(("batch", "gx"), "gy", None, None),
        P(),
        P(),
        P(),
        P(),
        P(),
        P(("batch", "gx"), "gy", None, None),
    )
    return jax.shard_map(
        local,
        mesh=mesh,
        in_specs=placed,
        out_specs=(
            P(("batch", "gx"), "gy", None, None),
            P(("batch", "gx", "gy"), None),
            P(("batch", "gx", "gy"), None),
            P(("batch", "gx", "gy")),
            P(("batch", "gx", "gy"), None),
            P(("batch", "gx", "gy"), None),
        ),
        check_vma=False,
    )
```

time: 552 us -> 373 us (0.68); the launches traced: 544 us -> 372 us
  waiting for transfers between devices: 293 us -> 176 us
  local copies, waits for them, and re-layouts: 90.6 us -> 39 us
  Pallas kernels: 0 us -> 51.4 us
  matrix products: 78.3 us -> 33.5 us
  other arithmetic: 17.6 us -> 9 us
    all_gather x2 -> x0, waiting for transfers between devices: 68.6 us -> none  [the longest x1 39.4 us: local(): lax.all_gather(local_keys, ('gx', 'gy'), axis=0, tiled=True)]
    unnamed x8 -> x4, waiting for transfers between devices: 52.5 us -> 0.07 us
    pallas_call x0 -> x1, Pallas kernels: none -> 51.4 us  [attention(): pl.pallas_call(functools.partial(attention_kernel, n, n_gy), out_shape=(j...]
    dot_general x17 -> x12, matrix products: 78.3 us -> 33.5 us  [the longest x1 10.7 us: local(): lax.dot_general(patches, d_hidden, tn, preferred_element_type=F32)]
    all_gather x0 -> x1, blocking collectives: none -> 33.1 us  [reduce_all(): gains = lax.all_gather(gain_part, ('gx', 'gy'), axis=0)]
    unnamed x1 -> x0, blocking collectives: 32.6 us -> none
    unnamed x74 -> x77, local copies, waits for them, and re-layouts: 38.3 us -> 10.7 us
    reshape x5 -> x7, local copies, waits for them, and re-layouts: 27.1 us -> 3.85 us  [the longest x1 1.2 us: local(): grad_features.reshape(z, x, y, channels).transpose(1, 2, 0, 3)]
  transfers between devices with their start and end apart: 15 -> 12, of which waited for: 10 -> 6; matrix products, arithmetic and copies ran while one was open for 16% -> 14% of each run, Pallas kernels for 0% -> 0%
where the time goes in v1:
time: 373 us; the launch traced here: 372 us
  waiting for transfers between devices  176 us (47%)
  Pallas kernels  51.4 us (14%)
  local copies, waits for them, and re-layouts  39 us (10%)
  matrix products  33.5 us (9%)
  blocking collectives  33.1 us (9%)
  starting transfers between devices  15.8 us (4%)
  between operations  14.6 us (4%)
  other arithmetic  9 us (2%)
    reduce_scatter x4, waiting for transfers between devices, scatter(): return lax.psum_scatter(part, ('gx', 'gy'), scatter_dimension=0, tiled=True)  168 us
    pallas_call x1, Pallas kernels, attention(): pl.pallas_call(functools.partial(attention_kernel, n, n_gy), out_shape=(j...  51.4 us
    all_gather x1, blocking collectives, reduce_all(): gains = lax.all_gather(gain_part, ('gx', 'gy'), axis=0)  33.1 us
    unnamed x77, local copies, waits for them, and re-layouts  10.7 us
    dot_general x1, matrix products, local(): lax.dot_general(patches, d_hidden, tn, preferred_element_type=F32)  10.7 us
    ppermute x4, starting transfers between devices, halo(): lax.ppermute(lax.slice_in_dim(block, block.shape[dim] - 1, None, axis=dim...  10.3 us
  transfers between devices with their start and end apart: 12, of which 6 were waited for; matrix products, arithmetic and copies ran while one was open for 14% of the time, Pallas kernels for 0%

profile of v1, /device:TPU:0, one launch (start us, length us, event | category | flops | bytes accessed | tf_op | source)
XLA Modules:
  0.0 372.1 jit_solution(15208060364107705558)
XLA Ops:
  8.6 2.4 collective-permute-start
  13.2 2.9 collective-permute-done.1
  16.9 4.1 %collective-permute-start.2 = (bf16[4,18,1,256]{3,2,1,0:T(2,128)(2,1)}, bf16[4,18,1,256]{3,2,1,0:T(2,128)(2,1)}, u32[]{:S(2)}, u32[]{:S(2)}) collective-permute-start(bf16[4,18,1,256]{3,2,1,0:T(2,128)(2,1)} %get-tuple-element.43), channel_id=1, source_target_pairs={{0,1},{1,2},{2,3},{4,5},{5,6},{6,7},{8,9},{9,10},{10,11},{12,13},{... | collective-permute-start | bytes 110600 | tf_op jit(solution)/shard_map/ppermute | solution.py:22
  25.6 2.3 slice.331
  27.9 2.3 copy.64
  30.2 2.3 copy.54
  34.0 1.5 pad_maximum_fusion
  40.1 5.2 %multiply_convert_fusion.1 = (bf16[1024,256]{1,0:T(8,128)(2,1)S(1)}, f32[1024,256]{1,0:T(8,128)}) fusion(bf16[1024,6912]{1,0:T(8,128)(2,1)S(1)} %bitcast.141, bf16[6912,256]{1,0:T(8,128)(2,1)S(1)} %copy-done.2), kind=kOutput, calls=%fused_computation.36 | convolution fusion | flops 3625189376 | bytes 19267584 | tf_op jit(solution)/shard_map/dot_general | solution.py:215
  50.8 1.7 fusion.20
  52.9 51.4 %shard_map.118 = (bf16[8,128,128]{2,1,0:T(8,128)(2,1)S(1)}, bf16[8,128,128]{2,1,0:T(8,128)(2,1)S(1)}) custom-call(bf16[16,192,128]{2,1,0:T(8,128)(2,1)S(1)} %bitcast.86), custom_call_target="tpu_custom_call" | custom-call | flops 2000000000 | bytes 2000000 | tf_op jit(solution)/shard_map/pallas_call | solution.py:178
  106.2 2.8 convolution_convert_fusion.2
  113.4 2.0 multiply_reduce_fusion
  115.6 2.1 convolution_convert_fusion.1
  117.8 5.8 %copy.59 = bf16[27,256,256]{2,1,0:T(8,128)(2,1)} copy(bf16[27,256,256]{1,2,0:T(8,128)(2,1)} %bitcast.103) | data formatting | bytes 7077888 | tf_op jit(solution)/shard_map/transpose | solution.py:274
  126.6 1.6 multiply_convert_fusion
  128.2 2.5 collective-permute-start.4
  132.3 10.7 %convolution_convert_fusion = bf16[6912,256]{1,0:T(8,128)(2,1)} fusion(bf16[1024,6912]{1,0:T(8,128)(2,1)} %bitcast.142, bf16[1024,256]{1,0:T(8,128)(2,1)S(1)} %multiply_convert_fusion), kind=kOutput, calls=%fused_computation | convolution fusion | flops 3625648128 | bytes 18219008 | tf_op jit(solution)/shard_map/dot_general | solution.py:268
  143.0 33.1 %all-gather.1 = f32[16,1,512]{2,1,0:T(1,128)S(1)} all-gather(f32[1,1,512]{2,1,0:T(1,128)S(1)} %bitcast.143), channel_id=2, replica_groups=mesh['batch'=2,'gx'=4,'gy'=4] {'gx','gy'}, dimensions={0}, use_global_device_ids=true | all-gather | bytes 34816 | tf_op jit(solution)/shard_map/all_gather | solution.py:292
  180.2 4.3 %collective-permute-done.7 = bf16[4,18,1,256]{3,2,1,0:T(2,128)(2,1)S(1)} collective-permute-done((bf16[4,18,1,256]{3,2,1,0:T(2,128)(2,1)S(1)}, bf16[4,18,1,256]{3,2,1,0:T(2,128)(2,1)S(1)}, u32[]{:S(2)}, u32[]{:S(2)}) %collective-permute-start.7) | collective-permute-done | bytes 36896 | tf_op jit(solution)/shard_map/ppermute | solution.py:25
  185.1 2.3 fusion.26
  190.3 3.8 %convolution_convert_fusion.4 = bf16[1024,256]{1,0:T(8,128)(2,1)S(1)} fusion(bf16[1024,6912]{1,0:T(8,128)(2,1)S(1)} %constant_dynamic-update-slice_fusion.1, bf16[6912,256]{1,0:T(8,128)(2,1)S(1)} %bitcast.104), kind=kOutput, calls=%fused_computation.28 | convolution fusion | flops 3624140800 | bytes 18219008 | tf_op jit(solution)/shard_map/dot_general | solution.py:277
  197.9 30.9 %reduce-scatter.11.cloned.1.call-done = bf16[32,512]{1,0:T(8,128)(2,1)} async-done(((bf16[512,512]{1,0:T(8,128)(2,1)}), bf16[32,512]{1,0:T(8,128)(2,1)}) %reduce-scatter.11.cloned.1.call-update) | async-done | bytes 32784 | tf_op jit(solution)/shard_map/reduce_scatter | solution.py:290
  228.7 64.9 %reduce-scatter.7.cloned.1.call-done = bf16[128,512]{1,0:T(8,128)(2,1)} async-done(((bf16[2048,512]{1,0:T(8,128)(2,1)}), bf16[128,512]{1,0:T(8,128)(2,1)}) %reduce-scatter.7.cloned.1.call-update) | async-done | bytes 131088 | tf_op jit(solution)/shard_map/reduce_scatter | solution.py:290
  293.6 72.0 %reduce-scatter.5.cloned.1.call-done = bf16[432,256]{1,0:T(8,128)(2,1)} async-done(((bf16[6912,256]{1,0:T(8,128)(2,1)}), bf16[432,256]{1,0:T(8,128)(2,1)}) %reduce-scatter.5.cloned.1.call-update) | async-done | bytes 221200 | tf_op jit(solution)/shard_map/reduce_scatter | solution.py:290
  (148 shorter events, 42.6 us)
Async XLA Ops:
  7.2 39.6 %copy-start = (bf16[2048,512]{1,0:T(8,128)(2,1)S(1)}, bf16[2048,512]{1,0:T(8,128)(2,1)}, u32[]{:S(2)}) copy-start(bf16[2048,512]{1,0:T(8,128)(2,1)} %param.9) | copy-start | bytes 6291460
  7.2 30.8 %copy-start.4 = (bf16[16,16,4,256]{3,2,1,0:T(4,128)(2,1)S(1)}, bf16[16,16,4,256]{3,2,1,0:T(4,128)(2,1)}, u32[]{:S(2)}) copy-start(bf16[16,16,4,256]{3,2,1,0:T(4,128)(2,1)} %param.7) | copy-start | bytes 1572868
  7.2 188.1 %reduce-scatter.9.cloned.1.call-start = ((), (), s32[]{:S(2)}) async-start(), calls=%async_computation.6 | async-start | bytes 1671168 | tf_op jit(solution)/shard_map/reduce_scatter | solution.py:290
  8.6 4.6 %collective-permute-start = (bf16[4,1,16,256]{3,2,1,0:T(8,128)(2,1)S(1)}, bf16[4,1,16,256]{3,2,1,0:T(8,128)(2,1)S(1)}, u32[]{:S(2)}, u32[]{:S(2)}) collective-permute-start(bf16[4,1,16,256]{3,2,1,0:T(8,128)(2,1)S(1)} %get-tuple-element.49), channel_id=1, source_target_pairs={{0,4},{4,8},{8,12},{1,5},{5,9},{9,13},{2,6},{6,10},{10,14},{3,7},{... | collective-permute-start | bytes 98312 | tf_op jit(solution)/shard_map/ppermute | solution.py:22
  10.9 5.2 %collective-permute-start.1 = (bf16[4,1,16,256]{3,2,1,0:T(8,128)(2,1)S(1)}, bf16[4,1,16,256]{3,2,1,0:T(8,128)(2,1)S(1)}, u32[]{:S(2)}, u32[]{:S(2)}) collective-permute-start(bf16[4,1,16,256]{3,2,1,0:T(8,128)(2,1)S(1)} %get-tuple-element.50), channel_id=1, source_target_pairs={{4,0},{8,4},{12,8},{5,1},{9,5},{13,9},{6,2},{10,6},{14,10},{7,3},{... | collective-permute-start | bytes 98312 | tf_op jit(solution)/shard_map/ppermute | solution.py:25
  13.2 10.5 %copy-start.7 = (bf16[4,1,16,256]{3,2,1,0:T(8,128)(2,1)}, bf16[4,1,16,256]{3,2,1,0:T(8,128)(2,1)S(1)}, u32[]{:S(2)}) copy-start(bf16[4,1,16,256]{3,2,1,0:T(8,128)(2,1)S(1)} %collective-permute-done) | copy-start | bytes 98308
  16.2 7.5 %copy-start.5 = (bf16[4,1,16,256]{3,2,1,0:T(8,128)(2,1)}, bf16[4,1,16,256]{3,2,1,0:T(8,128)(2,1)S(1)}, u32[]{:S(2)}) copy-start(bf16[4,1,16,256]{3,2,1,0:T(8,128)(2,1)S(1)} %collective-permute-done.1) | copy-start | bytes 98308
  16.9 15.5 %collective-permute-start.2 = (bf16[4,18,1,256]{3,2,1,0:T(2,128)(2,1)}, bf16[4,18,1,256]{3,2,1,0:T(2,128)(2,1)}, u32[]{:S(2)}, u32[]{:S(2)}) collective-permute-start(bf16[4,18,1,256]{3,2,1,0:T(2,128)(2,1)} %get-tuple-element.43), channel_id=1, source_target_pairs={{0,1},{1,2},{2,3},{4,5},{5,6},{6,7},{8,9},{9,10},{10,11},{12,13},{... | collective-permute-start | bytes 110600 | tf_op jit(solution)/shard_map/ppermute | solution.py:22
  21.0 11.4 %collective-permute-start.3 = (bf16[4,18,1,256]{3,2,1,0:T(2,128)(2,1)}, bf16[4,18,1,256]{3,2,1,0:T(2,128)(2,1)}, u32[]{:S(2)}, u32[]{:S(2)}) collective-permute-start(bf16[4,18,1,256]{3,2,1,0:T(2,128)(2,1)} %get-tuple-element.44), channel_id=1, source_target_pairs={{1,0},{2,1},{3,2},{5,4},{6,5},{7,6},{9,8},{10,9},{11,10},{13,12},{... | collective-permute-start | bytes 110600 | tf_op jit(solution)/shard_map/ppermute | solution.py:25
  32.5 6.8 %copy-start.6 = (bf16[4,1,16,256]{3,2,1,0:T(8,128)(2,1)S(1)}, bf16[4,1,16,256]{3,2,1,0:T(8,128)(2,1)}, u32[]{:S(2)}) copy-start(bf16[4,1,16,256]{3,2,1,0:T(8,128)(2,1)} %copy-done.5) | copy-start | bytes 98308
  35.6 4.6 %copy-start.2 = (bf16[6912,256]{1,0:T(8,128)(2,1)S(1)}, bf16[6912,256]{1,0:T(8,128)(2,1)}, u32[]{:S(2)}) copy-start(bf16[6912,256]{1,0:T(8,128)(2,1)} %param.8) | copy-start | bytes 10616836
  40.1 5.3 %copy-start.9 = (bf16[4,16,16,6912]{3,2,1,0:T(8,128)(2,1)}, bf16[4,16,16,6912]{3,2,1,0:T(8,128)(2,1)S(1)}, u32[]{:S(2)}) copy-start(bf16[4,16,16,6912]{3,2,1,0:T(8,128)(2,1)S(1)} %slice_dynamic-update-slice_fusion) | copy-start | bytes 42467332
  40.1 7.4 %copy-start.10 = (f32[512]{0:T(512)S(1)}, f32[512]{0:T(512)}, u32[]{:S(2)}) copy-start(f32[512]{0:T(512)} %param.10) | copy-start | bytes 6148
  106.1 2.9 copy-start.8
  109.0 119.7 %reduce-scatter.11.cloned.1.call-start = ((), (), s32[]{:S(2)}) async-start(), calls=%async_computation.7 | async-start | bytes 557056 | tf_op jit(solution)/shard_map/reduce_scatter | solution.py:290
  113.4 180.2 %reduce-scatter.7.cloned.1.call-start = ((), (), s32[]{:S(2)}) async-start(), calls=%async_computation.5 | async-start | bytes 2228224 | tf_op jit(solution)/shard_map/reduce_scatter | solution.py:290
  117.8 247.8 %reduce-scatter.5.cloned.1.call-start = ((), (), s32[]{:S(2)}) async-start(), calls=%async_computation.4 | async-start | bytes 3760128 | tf_op jit(solution)/shard_map/reduce_scatter | solution.py:290
  128.2 48.5 %collective-permute-start.4 = (bf16[4,1,16,256]{3,2,1,0:T(8,128)(2,1)S(1)}, bf16[4,1,16,256]{3,2,1,0:T(8,128)(2,1)S(1)}, u32[]{:S(2)}, u32[]{:S(2)}) collective-permute-start(bf16[4,1,16,256]{3,2,1,0:T(8,128)(2,1)S(1)} %get-tuple-element.47), channel_id=1, source_target_pairs={{0,4},{4,8},{8,12},{1,5},{5,9},{9,13},{2,6},{6,10},{10,14},{3,7},{... | collective-permute-start | bytes 98312 | tf_op jit(solution)/shard_map/ppermute | solution.py:22
  130.8 46.0 %collective-permute-start.5 = (bf16[4,1,16,256]{3,2,1,0:T(8,128)(2,1)S(1)}, bf16[4,1,16,256]{3,2,1,0:T(8,128)(2,1)S(1)}, u32[]{:S(2)}, u32[]{:S(2)}) collective-permute-start(bf16[4,1,16,256]{3,2,1,0:T(8,128)(2,1)S(1)} %get-tuple-element.48), channel_id=1, source_target_pairs={{4,0},{8,4},{12,8},{5,1},{9,5},{13,9},{6,2},{10,6},{14,10},{7,3},{... | collective-permute-start | bytes 98312 | tf_op jit(solution)/shard_map/ppermute | solution.py:25
  176.9 3.3 collective-permute-start.6
  178.2 6.2 %collective-permute-start.7 = (bf16[4,18,1,256]{3,2,1,0:T(2,128)(2,1)S(1)}, bf16[4,18,1,256]{3,2,1,0:T(2,128)(2,1)S(1)}, u32[]{:S(2)}, u32[]{:S(2)}) collective-permute-start(bf16[4,18,1,256]{3,2,1,0:T(2,128)(2,1)S(1)} %get-tuple-element.40), channel_id=1, source_target_pairs={{1,0},{2,1},{3,2},{5,4},{6,5},{7,6},{9,8},{10,9},{11,10},{13,12},{... | collective-permute-start | bytes 110600 | tf_op jit(solution)/shard_map/ppermute | solution.py:25
  188.2 2.0 copy-start.3
  189.4 176.1 %copy-start.1 = (bf16[2048,512]{1,0:T(8,128)(2,1)S(1)}, bf16[2048,512]{1,0:T(8,128)(2,1)}, u32[]{:S(2)}) copy-start(bf16[2048,512]{1,0:T(8,128)(2,1)} %param.9) | copy-start | bytes 6291460
Sparse Core Ops, SparseCore 0:
  109.1 60.2 reduce-scatter.8
  173.9 54.7 reduce-scatter.10
  233.1 60.5 reduce-scatter.6
  298.4 67.1 reduce-scatter.4

commit v2 on v1

--- a/solution.py
+++ b/solution.py
@@ -285,15 +285,55 @@
     return grad_features, conv_sum, down_sum, gain_sum, qkv_sum, out_sum
 
 
+CORE = ("gx", 1, 1)
+Y = ("gx", 2, 0)
+Z_NEAR = ("gy", 1, 3)
+Z_FAR = ("gy", 2, 2)
+
+
+def swap(array, axis, step):
+    pairs = [(i, i ^ step) for i in range(lax.axis_size(axis))]
+    return lax.ppermute(array, axis, pairs)
+
+
+def halve(part, side):
+    axis, step, dim = side
+    bit = lax.rem(lax.axis_index(axis) // step, 2)
+    kept = lax.dynamic_slice_in_dim(part, bit, 1, dim)
+    sent = lax.dynamic_slice_in_dim(part, 1 - bit, 1, dim)
+    return (kept.astype(F32) + swap(sent, axis, step).astype(F32)).astype(part.dtype)
+
+
+def scatter(part, sides):
+    for side in sides:
+        part = halve(part, side)
+    return part.reshape(part.shape[4:])
+
+
 def reduce_all(conv_part, down_part, qkv_part, out_part, gain_part):
-    def scatter(part):
-        return lax.psum_scatter(part, ("gx", "gy"), scatter_dimension=0, tiled=True)
-
-    gains = lax.all_gather(gain_part, ("gx", "gy"), axis=0)
+    group = lax.axis_size("gx") * lax.axis_size("gy")
+    width = out_part.shape[1]
+    chunked = [part.reshape(group, -1, part.shape[1]) for part in (out_part, down_part, qkv_part)]
+    thirds = [chunked[2][:, :, i * width : (i + 1) * width] for i in range(3)]
+    early = jnp.concatenate(chunked[:2] + thirds, axis=1)
+    early = scatter(
+        early.reshape((2, 2, 2, 2) + early.shape[1:]), (CORE, Y, Z_NEAR, Z_FAR)
+    )
+    rows = chunked[0].shape[1]
+    down_rows = chunked[1].shape[1]
+    out_sum = early[:rows]
+    down_sum = early[rows : rows + down_rows]
+    third = early[rows + down_rows :].reshape(3, rows, width)
+    qkv_sum = jnp.concatenate([third[0], third[1], third[2]], axis=1)
+    conv_sum = scatter(
+        conv_part.reshape(2, 2, 2, 2, -1, conv_part.shape[1]), (CORE, Z_NEAR, Z_FAR, Y)
+    )
+    for axis, step, _ in (CORE, Y, Z_NEAR, Z_FAR):
+        gain_part = gain_part + swap(gain_part, axis, step)
+    size = gain_part.shape[0] // group
     me = lax.axis_index(("gx", "gy"))
-    size = gain_part.shape[0] // gains.shape[0]
-    gain_sum = lax.dynamic_slice_in_dim(jnp.sum(gains, axis=0), me * size, size, 0)
-    return scatter(conv_part), scatter(down_part), scatter(qkv_part), scatter(out_part), gain_sum
+    gain_sum = lax.dynamic_slice_in_dim(gain_part, me * size, size, 0)
+    return conv_sum, down_sum, qkv_sum, out_sum, gain_sum
 
 
 def solution(mesh):

time: 373 us -> 238 us (0.64)
  waiting for transfers between devices: 176 us -> 40.1 us
  blocking collectives: 33.1 us -> 0 us
  local copies, waits for them, and re-layouts: 39 us -> 66.7 us
  starting transfers between devices: 15.8 us -> 31.5 us
  between operations: 14.6 us -> 1.51 us
    reduce_scatter x4 -> x0, waiting for transfers between devices: 168 us -> none  [scatter(): return lax.psum_scatter(part, ('gx', 'gy'), scatter_dimension=0, tiled=True)]
    all_gather x1 -> x0, blocking collectives: 33.1 us -> none  [reduce_all(): gains = lax.all_gather(gain_part, ('gx', 'gy'), axis=0)]
    ppermute x0 -> x12, waiting for transfers between devices: none -> 31.6 us  [swap(): return lax.ppermute(array, axis, pairs)]
    unnamed x77 -> x96, local copies, waits for them, and re-layouts: 10.7 us -> 34.7 us
    ppermute x0 -> x12, starting transfers between devices: none -> 15.6 us  [swap(): return lax.ppermute(array, axis, pairs)]
  transfers between devices with their start and end apart: 12 -> 20, of which waited for: 6 -> 9; matrix products, arithmetic and copies ran while one was open for 14% -> 31% of each run, Pallas kernels for 0% -> 0%
where the time goes in v2:
time: 238 us; the launch traced here: 237 us
  local copies, waits for them, and re-layouts  66.7 us (28%)
  Pallas kernels  51.4 us (22%)
  waiting for transfers between devices  40.1 us (17%)
  matrix products  33.3 us (14%)
  starting transfers between devices  31.5 us (13%)
  other arithmetic  12.4 us (5%)
    pallas_call x1, Pallas kernels, attention(): pl.pallas_call(functools.partial(attention_kernel, n, n_gy), out_shape=(j...  51.4 us
    unnamed x96, local copies, waits for them, and re-layouts  34.7 us
    ppermute x12, waiting for transfers between devices, swap(): return lax.ppermute(array, axis, pairs)  31.6 us
    ppermute x12, starting transfers between devices, swap(): return lax.ppermute(array, axis, pairs)  15.6 us
    ppermute x4, starting transfers between devices, halo(): lax.ppermute(lax.slice_in_dim(block, block.shape[dim] - 1, None, axis=dim...  10.5 us
    dot_general x1, matrix products, local(): lax.dot_general(patches, d_hidden, tn, preferred_element_type=F32)  8.93 us
    ppermute x4, waiting for transfers between devices, halo(): high = lax.ppermute(lax.slice_in_dim(block, 0, 1, axis=dim), axis, backward)  7.86 us
    dot_general x1, matrix products, local(): jnp.dot(d_patches, conv_flip, preferred_element_type=F32).astype(BF)  7.37 us
  transfers between devices with their start and end apart: 20, of which 9 were waited for; matrix products, arithmetic and copies ran while one was open for 31% of the time, Pallas kernels for 0%

profile of v2, /device:TPU:0, one launch (start us, length us, event | category | flops | bytes accessed | tf_op | source)
XLA Modules:
  0.0 236.9 jit_solution(16491943370959013290)
XLA Ops:
  1.9 2.4 collective-permute-start
  6.6 2.9 %collective-permute-done.1 = bf16[4,1,16,256]{3,2,1,0:T(8,128)(2,1)S(1)} collective-permute-done((bf16[4,1,16,256]{3,2,1,0:T(8,128)(2,1)S(1)}, bf16[4,1,16,256]{3,2,1,0:T(8,128)(2,1)S(1)}, u32[]{:S(2)}, u32[]{:S(2)}) %collective-permute-start.1) | collective-permute-done | bytes 32800 | tf_op jit(solution)/shard_map/ppermute | solution.py:25
  10.3 4.1 %collective-permute-start.2 = (bf16[4,18,1,256]{3,2,1,0:T(2,128)(2,1)}, bf16[4,18,1,256]{3,2,1,0:T(2,128)(2,1)}, u32[]{:S(2)}, u32[]{:S(2)}) collective-permute-start(bf16[4,18,1,256]{3,2,1,0:T(2,128)(2,1)} %get-tuple-element.46), channel_id=1, source_target_pairs={{0,1},{1,2},{2,3},{4,5},{5,6},{6,7},{8,9},{9,10},{10,11},{12,13},{... | collective-permute-start | bytes 110600 | tf_op jit(solution)/shard_map/ppermute | solution.py:22
  15.7 2.0 convolution_convert_fusion.7
  17.7 2.3 slice.363
  21.9 2.3 copy.49
  24.2 2.3 copy.39
  27.5 5.8 %copy.44 = bf16[27,256,256]{2,1,0:T(8,128)(2,1)} copy(bf16[27,256,256]{1,2,0:T(8,128)(2,1)} %bitcast.124) | data formatting | bytes 7077888 | tf_op jit(solution)/shard_map/transpose | solution.py:274
  40.8 4.8 %multiply_convert_fusion.1 = (bf16[1024,256]{1,0:T(8,128)(2,1)S(1)}, f32[1024,256]{1,0:T(8,128)}) fusion(bf16[1024,6912]{1,0:T(8,128)(2,1)S(1)} %bitcast.167, bf16[6912,256]{1,0:T(8,128)(2,1)S(1)} %copy-done.5), kind=kOutput, calls=%fused_computation.41 | convolution fusion | flops 3625189376 | bytes 19267584 | tf_op jit(solution)/shard_map/dot_general | solution.py:215
  53.2 51.4 %shard_map.118 = (bf16[8,128,128]{2,1,0:T(8,128)(2,1)S(1)}, bf16[8,128,128]{2,1,0:T(8,128)(2,1)S(1)}) custom-call(bf16[16,192,128]{2,1,0:T(8,128)(2,1)S(1)} %bitcast.105), custom_call_target="tpu_custom_call" | custom-call | flops 2000000000 | bytes 2000000 | tf_op jit(solution)/shard_map/pallas_call | solution.py:178
  110.1 2.0 convolution_convert_fusion.1
  116.6 2.0 copy-done.3
  125.8 8.9 %convolution_convert_fusion = bf16[6912,256]{1,0:T(8,128)(2,1)S(1)} fusion(bf16[1024,6912]{1,0:T(8,128)(2,1)} %bitcast.168, bf16[1024,256]{1,0:T(8,128)(2,1)S(1)} %multiply_convert_fusion), kind=kOutput, calls=%fused_computation | convolution fusion | flops 3625648128 | bytes 18219008 | tf_op jit(solution)/shard_map/dot_general | solution.py:268
  139.2 2.7 %collective-permute-start.19 = (f32[512]{0:T(512)S(1)}, f32[512]{0:T(512)S(1)}, u32[]{:S(2)}, u32[]{:S(2)}) collective-permute-start(f32[512]{0:T(512)S(1)} %add.129), channel_id=1, source_target_pairs={{0,2},{1,3},{2,0},{3,1},{4,6},{5,7},{6,4},{7,5},{8,10},{9,11},{10,... | collective-permute-start | bytes 6152 | tf_op jit(solution)/shard_map/ppermute | solution.py:296
  144.5 2.6 %collective-permute-start.6 = (bf16[4,18,1,256]{3,2,1,0:T(2,128)(2,1)S(1)}, bf16[4,18,1,256]{3,2,1,0:T(2,128)(2,1)S(1)}, u32[]{:S(2)}, u32[]{:S(2)}) collective-permute-start(bf16[4,18,1,256]{3,2,1,0:T(2,128)(2,1)S(1)} %get-tuple-element.42), channel_id=1, source_target_pairs={{0,1},{1,2},{2,3},{4,5},{5,6},{6,7},{8,9},{9,10},{10,11},{12,13},{... | collective-permute-start | bytes 110600 | tf_op jit(solution)/shard_map/ppermute | solution.py:22
  149.5 4.9 %collective-permute-done.7 = bf16[4,18,1,256]{3,2,1,0:T(2,128)(2,1)S(1)} collective-permute-done((bf16[4,18,1,256]{3,2,1,0:T(2,128)(2,1)S(1)}, bf16[4,18,1,256]{3,2,1,0:T(2,128)(2,1)S(1)}, u32[]{:S(2)}, u32[]{:S(2)}) %collective-permute-start.7) | collective-permute-done | bytes 36896 | tf_op jit(solution)/shard_map/ppermute | solution.py:25
  155.8 2.1 fusion.28
  177.0 2.2 add_convert_fusion
  179.3 3.3 %collective-permute-start.13 = (bf16[1,1,2,2,256,512]{5,4,3,2,1,0:T(8,128)(2,1)S(1)}, bf16[1,1,2,2,256,512]{5,4,3,2,1,0:T(8,128)(2,1)S(1)}, u32[]{:S(2)}, u32[]{:S(2)}) collective-permute-start(bf16[1,1,2,2,256,512]{5,4,3,2,1,0:T(8,128)(2,1)S(1)} %constant_dynamic-slice_fusion.2), channel_id=1, source_target_pairs={{0,8},{4,12},{8,0},{12,4},{1,9},{5,13},{9,1},{13,5},{2,10},{6,14},... | collective-permute-start | bytes 3145736 | tf_op jit(solution)/shard_map/ppermute | solution.py:296
  188.0 8.6 %collective-permute-done.9 = bf16[2,1,2,1,432,256]{5,4,3,2,1,0:T(8,128)(2,1)S(1)} collective-permute-done((bf16[2,1,2,1,432,256]{5,4,3,2,1,0:T(8,128)(2,1)S(1)}, bf16[2,1,2,1,432,256]{5,4,3,2,1,0:T(8,128)(2,1)S(1)}, u32[]{:S(2)}, u32[]{:S(2)}) %collective-permute-start.9) | collective-permute-done | bytes 884768 | tf_op jit(solution)/shard_map/ppermute | solution.py:296
  198.2 5.6 %collective-permute-done.13 = bf16[1,1,2,2,256,512]{5,4,3,2,1,0:T(8,128)(2,1)S(1)} collective-permute-done((bf16[1,1,2,2,256,512]{5,4,3,2,1,0:T(8,128)(2,1)S(1)}, bf16[1,1,2,2,256,512]{5,4,3,2,1,0:T(8,128)(2,1)S(1)}, u32[]{:S(2)}, u32[]{:S(2)}) %collective-permute-start.13) | collective-permute-done | bytes 1048608 | tf_op jit(solution)/shard_map/ppermute | solution.py:296
  207.2 11.4 %collective-permute-done.10 = bf16[2,1,1,1,432,256]{5,4,3,2,1,0:T(8,128)(2,1)S(1)} collective-permute-done((bf16[2,1,1,1,432,256]{5,4,3,2,1,0:T(8,128)(2,1)S(1)}, bf16[2,1,1,1,432,256]{5,4,3,2,1,0:T(8,128)(2,1)S(1)}, u32[]{:S(2)}, u32[]{:S(2)}) %collective-permute-start.10) | collective-permute-done | bytes 442400 | tf_op jit(solution)/shard_map/ppermute | solution.py:296
  218.8 5.1 %collective-permute-done.14 = bf16[1,1,2,1,256,512]{5,4,3,2,1,0:T(8,128)(2,1)S(1)} collective-permute-done((bf16[1,1,2,1,256,512]{5,4,3,2,1,0:T(8,128)(2,1)S(1)}, bf16[1,1,2,1,256,512]{5,4,3,2,1,0:T(8,128)(2,1)S(1)}, u32[]{:S(2)}, u32[]{:S(2)}) %collective-permute-start.14) | collective-permute-done | bytes 524320 | tf_op jit(solution)/shard_map/ppermute | solution.py:296
  224.2 7.4 %convolution_convert_fusion.4 = bf16[1024,256]{1,0:T(8,128)(2,1)S(1)} fusion(bf16[1024,6912]{1,0:T(8,128)(2,1)} %constant_dynamic-update-slice_fusion.1, bf16[6912,256]{1,0:T(8,128)(2,1)S(1)} %bitcast.125), kind=kOutput, calls=%fused_computation.32 | convolution fusion | flops 3624140800 | bytes 18219008 | tf_op jit(solution)/shard_map/dot_general | solution.py:277
  (201 shorter events, 86.4 us)
Async XLA Ops:
  0.6 46.4 %copy-start = (bf16[2048,512]{1,0:T(8,128)(2,1)S(1)}, bf16[2048,512]{1,0:T(8,128)(2,1)}, u32[]{:S(2)}) copy-start(bf16[2048,512]{1,0:T(8,128)(2,1)} %param.9) | copy-start | bytes 6291460
  1.9 4.6 %collective-permute-start = (bf16[4,1,16,256]{3,2,1,0:T(8,128)(2,1)S(1)}, bf16[4,1,16,256]{3,2,1,0:T(8,128)(2,1)S(1)}, u32[]{:S(2)}, u32[]{:S(2)}) collective-permute-start(bf16[4,1,16,256]{3,2,1,0:T(8,128)(2,1)S(1)} %get-tuple-element.52), channel_id=1, source_target_pairs={{0,4},{4,8},{8,12},{1,5},{5,9},{9,13},{2,6},{6,10},{10,14},{3,7},{... | collective-permute-start | bytes 98312 | tf_op jit(solution)/shard_map/ppermute | solution.py:22
  4.3 5.2 %collective-permute-start.1 = (bf16[4,1,16,256]{3,2,1,0:T(8,128)(2,1)S(1)}, bf16[4,1,16,256]{3,2,1,0:T(8,128)(2,1)S(1)}, u32[]{:S(2)}, u32[]{:S(2)}) collective-permute-start(bf16[4,1,16,256]{3,2,1,0:T(8,128)(2,1)S(1)} %get-tuple-element.53), channel_id=1, source_target_pairs={{4,0},{8,4},{12,8},{5,1},{9,5},{13,9},{6,2},{10,6},{14,10},{7,3},{... | collective-permute-start | bytes 98312 | tf_op jit(solution)/shard_map/ppermute | solution.py:25
  6.6 13.5 %copy-start.14 = (bf16[4,1,16,256]{3,2,1,0:T(8,128)(2,1)}, bf16[4,1,16,256]{3,2,1,0:T(8,128)(2,1)S(1)}, u32[]{:S(2)}) copy-start(bf16[4,1,16,256]{3,2,1,0:T(8,128)(2,1)S(1)} %collective-permute-done) | copy-start | bytes 98308
  10.3 22.9 %collective-permute-start.2 = (bf16[4,18,1,256]{3,2,1,0:T(2,128)(2,1)}, bf16[4,18,1,256]{3,2,1,0:T(2,128)(2,1)}, u32[]{:S(2)}, u32[]{:S(2)}) collective-permute-start(bf16[4,18,1,256]{3,2,1,0:T(2,128)(2,1)} %get-tuple-element.46), channel_id=1, source_target_pairs={{0,1},{1,2},{2,3},{4,5},{5,6},{6,7},{8,9},{9,10},{10,11},{12,13},{... | collective-permute-start | bytes 110600 | tf_op jit(solution)/shard_map/ppermute | solution.py:22
  14.4 18.8 %collective-permute-start.3 = (bf16[4,18,1,256]{3,2,1,0:T(2,128)(2,1)}, bf16[4,18,1,256]{3,2,1,0:T(2,128)(2,1)}, u32[]{:S(2)}, u32[]{:S(2)}) collective-permute-start(bf16[4,18,1,256]{3,2,1,0:T(2,128)(2,1)} %get-tuple-element.47), channel_id=1, source_target_pairs={{1,0},{2,1},{3,2},{5,4},{6,5},{7,6},{9,8},{10,9},{11,10},{13,12},{... | collective-permute-start | bytes 110600 | tf_op jit(solution)/shard_map/ppermute | solution.py:25
  120.2 56.7 %collective-permute-start.12 = (bf16[2,1,2,2,256,512]{5,4,3,2,1,0:T(8,128)(2,1)}, bf16[2,1,2,2,256,512]{5,4,3,2,1,0:T(8,128)(2,1)}, u32[]{:S(2)}, u32[]{:S(2)}) collective-permute-start(bf16[2,1,2,2,256,512]{5,4,3,2,1,0:T(8,128)(2,1)} %constant_dynamic-slice_fusion.3), channel_id=1, source_target_pairs={{0,4},{4,0},{8,12},{12,8},{1,5},{5,1},{9,13},{13,9},{2,6},{6,2},{1... | collective-permute-start | bytes 6291464 | tf_op jit(solution)/shard_map/ppermute | solution.py:296
  120.9 3.8 %collective-permute-start.16 = (f32[512]{0:T(512)S(1)}, f32[512]{0:T(512)S(1)}, u32[]{:S(2)}, u32[]{:S(2)}) collective-permute-start(f32[512]{0:T(512)S(1)} %get-tuple-element.10), channel_id=1, source_target_pairs={{0,4},{4,0},{8,12},{12,8},{1,5},{5,1},{9,13},{13,9},{2,6},{6,2},{1... | collective-permute-start | bytes 6152 | tf_op jit(solution)/shard_map/ppermute | solution.py:296
  124.6 10.1 %collective-permute-start.17 = (f32[512]{0:T(512)S(1)}, f32[512]{0:T(512)S(1)}, u32[]{:S(2)}, u32[]{:S(2)}) collective-permute-start(f32[512]{0:T(512)S(1)} %add.127), channel_id=1, source_target_pairs={{0,8},{4,12},{8,0},{12,4},{1,9},{5,13},{9,1},{13,5},{2,10},{6,14},... | collective-permute-start | bytes 6152 | tf_op jit(solution)/shard_map/ppermute | solution.py:296
  134.7 4.5 %collective-permute-start.18 = (f32[512]{0:T(512)S(1)}, f32[512]{0:T(512)S(1)}, u32[]{:S(2)}, u32[]{:S(2)}) collective-permute-start(f32[512]{0:T(512)S(1)} %add.128), channel_id=1, source_target_pairs={{0,1},{1,0},{2,3},{3,2},{4,5},{5,4},{6,7},{7,6},{8,9},{9,8},{10,11... | collective-permute-start | bytes 6152 | tf_op jit(solution)/shard_map/ppermute | solution.py:296
  136.4 7.9 %collective-permute-start.4 = (bf16[4,1,16,256]{3,2,1,0:T(8,128)(2,1)S(1)}, bf16[4,1,16,256]{3,2,1,0:T(8,128)(2,1)S(1)}, u32[]{:S(2)}, u32[]{:S(2)}) collective-permute-start(bf16[4,1,16,256]{3,2,1,0:T(8,128)(2,1)S(1)} %get-tuple-element.50), channel_id=1, source_target_pairs={{0,4},{4,8},{8,12},{1,5},{5,9},{9,13},{2,6},{6,10},{10,14},{3,7},{... | collective-permute-start | bytes 98312 | tf_op jit(solution)/shard_map/ppermute | solution.py:22
  137.9 6.5 %collective-permute-start.5 = (bf16[4,1,16,256]{3,2,1,0:T(8,128)(2,1)S(1)}, bf16[4,1,16,256]{3,2,1,0:T(8,128)(2,1)S(1)}, u32[]{:S(2)}, u32[]{:S(2)}) collective-permute-start(bf16[4,1,16,256]{3,2,1,0:T(8,128)(2,1)S(1)} %get-tuple-element.51), channel_id=1, source_target_pairs={{4,0},{8,4},{12,8},{5,1},{9,5},{13,9},{6,2},{10,6},{14,10},{7,3},{... | collective-permute-start | bytes 98312 | tf_op jit(solution)/shard_map/ppermute | solution.py:25
  139.2 4.5 %collective-permute-start.19 = (f32[512]{0:T(512)S(1)}, f32[512]{0:T(512)S(1)}, u32[]{:S(2)}, u32[]{:S(2)}) collective-permute-start(f32[512]{0:T(512)S(1)} %add.129), channel_id=1, source_target_pairs={{0,2},{1,3},{2,0},{3,1},{4,6},{5,7},{6,4},{7,5},{8,10},{9,11},{10,... | collective-permute-start | bytes 6152 | tf_op jit(solution)/shard_map/ppermute | solution.py:296
  142.0 32.7 %collective-permute-start.8 = (bf16[2,1,2,2,432,256]{5,4,3,2,1,0:T(8,128)(2,1)S(1)}, bf16[2,1,2,2,432,256]{5,4,3,2,1,0:T(8,128)(2,1)S(1)}, u32[]{:S(2)}, u32[]{:S(2)}) collective-permute-start(bf16[2,1,2,2,432,256]{5,4,3,2,1,0:T(8,128)(2,1)S(1)} %constant_dynamic-slice_fusion.7), channel_id=1, source_target_pairs={{0,4},{4,0},{8,12},{12,8},{1,5},{5,1},{9,13},{13,9},{2,6},{6,2},{1... | collective-permute-start | bytes 5308424 | tf_op jit(solution)/shard_map/ppermute | solution.py:296
  144.5 5.0 %collective-permute-start.6 = (bf16[4,18,1,256]{3,2,1,0:T(2,128)(2,1)S(1)}, bf16[4,18,1,256]{3,2,1,0:T(2,128)(2,1)S(1)}, u32[]{:S(2)}, u32[]{:S(2)}) collective-permute-start(bf16[4,18,1,256]{3,2,1,0:T(2,128)(2,1)S(1)} %get-tuple-element.42), channel_id=1, source_target_pairs={{0,1},{1,2},{2,3},{4,5},{5,6},{6,7},{8,9},{9,10},{10,11},{12,13},{... | collective-permute-start | bytes 110600 | tf_op jit(solution)/shard_map/ppermute | solution.py:22
  147.1 7.2 %collective-permute-start.7 = (bf16[4,18,1,256]{3,2,1,0:T(2,128)(2,1)S(1)}, bf16[4,18,1,256]{3,2,1,0:T(2,128)(2,1)S(1)}, u32[]{:S(2)}, u32[]{:S(2)}) collective-permute-start(bf16[4,18,1,256]{3,2,1,0:T(2,128)(2,1)S(1)} %get-tuple-element.43), channel_id=1, source_target_pairs={{1,0},{2,1},{3,2},{5,4},{6,5},{7,6},{9,8},{10,9},{11,10},{13,12},{... | collective-permute-start | bytes 110600 | tf_op jit(solution)/shard_map/ppermute | solution.py:25
  175.2 21.5 %collective-permute-start.9 = (bf16[2,1,2,1,432,256]{5,4,3,2,1,0:T(8,128)(2,1)S(1)}, bf16[2,1,2,1,432,256]{5,4,3,2,1,0:T(8,128)(2,1)S(1)}, u32[]{:S(2)}, u32[]{:S(2)}) collective-permute-start(bf16[2,1,2,1,432,256]{5,4,3,2,1,0:T(8,128)(2,1)S(1)} %constant_dynamic-slice_fusion.6), channel_id=1, source_target_pairs={{0,1},{1,0},{2,3},{3,2},{4,5},{5,4},{6,7},{7,6},{8,9},{9,8},{10,11... | collective-permute-start | bytes 2654216 | tf_op jit(solution)/shard_map/ppermute | solution.py:296
  179.3 24.5 %collective-permute-start.13 = (bf16[1,1,2,2,256,512]{5,4,3,2,1,0:T(8,128)(2,1)S(1)}, bf16[1,1,2,2,256,512]{5,4,3,2,1,0:T(8,128)(2,1)S(1)}, u32[]{:S(2)}, u32[]{:S(2)}) collective-permute-start(bf16[1,1,2,2,256,512]{5,4,3,2,1,0:T(8,128)(2,1)S(1)} %constant_dynamic-slice_fusion.2), channel_id=1, source_target_pairs={{0,8},{4,12},{8,0},{12,4},{1,9},{5,13},{9,1},{13,5},{2,10},{6,14},... | collective-permute-start | bytes 3145736 | tf_op jit(solution)/shard_map/ppermute | solution.py:296
  196.9 21.6 %collective-permute-start.10 = (bf16[2,1,1,1,432,256]{5,4,3,2,1,0:T(8,128)(2,1)S(1)}, bf16[2,1,1,1,432,256]{5,4,3,2,1,0:T(8,128)(2,1)S(1)}, u32[]{:S(2)}, u32[]{:S(2)}) collective-permute-start(bf16[2,1,1,1,432,256]{5,4,3,2,1,0:T(8,128)(2,1)S(1)} %constant_dynamic-slice_fusion.5), channel_id=1, source_target_pairs={{0,2},{1,3},{2,0},{3,1},{4,6},{5,7},{6,4},{7,5},{8,10},{9,11},{10,... | collective-permute-start | bytes 1327112 | tf_op jit(solution)/shard_map/ppermute | solution.py:296
  204.1 20.1 %copy-start.6 = (bf16[27,256,256]{2,1,0:T(8,128)(2,1)S(1)}, bf16[27,256,256]{2,1,0:T(8,128)(2,1)}, u32[]{:S(2)}) copy-start(bf16[27,256,256]{2,1,0:T(8,128)(2,1)} %copy.44) | copy-start | bytes 10616836
  204.1 19.8 %collective-permute-start.14 = (bf16[1,1,2,1,256,512]{5,4,3,2,1,0:T(8,128)(2,1)S(1)}, bf16[1,1,2,1,256,512]{5,4,3,2,1,0:T(8,128)(2,1)S(1)}, u32[]{:S(2)}, u32[]{:S(2)}) collective-permute-start(bf16[1,1,2,1,256,512]{5,4,3,2,1,0:T(8,128)(2,1)S(1)} %constant_dynamic-slice_fusion.1), channel_id=1, source_target_pairs={{0,1},{1,0},{2,3},{3,2},{4,5},{5,4},{6,7},{7,6},{8,9},{9,8},{10,11... | collective-permute-start | bytes 1572872 | tf_op jit(solution)/shard_map/ppermute | solution.py:296
  218.7 14.0 %collective-permute-start.11 = (bf16[1,1,1,1,432,256]{5,4,3,2,1,0:T(8,128)(2,1)S(1)}, bf16[1,1,1,1,432,256]{5,4,3,2,1,0:T(8,128)(2,1)S(1)}, u32[]{:S(2)}, u32[]{:S(2)}) collective-permute-start(bf16[1,1,1,1,432,256]{5,4,3,2,1,0:T(8,128)(2,1)S(1)} %constant_dynamic-slice_fusion.4), channel_id=1, source_target_pairs={{0,8},{4,12},{8,0},{12,4},{1,9},{5,13},{9,1},{13,5},{2,10},{6,14},... | collective-permute-start | bytes 663560 | tf_op jit(solution)/shard_map/ppermute | solution.py:296
  224.1 10.2 %collective-permute-start.15 = (bf16[1,1,1,1,256,512]{5,4,3,2,1,0:T(8,128)(2,1)S(1)}, bf16[1,1,1,1,256,512]{5,4,3,2,1,0:T(8,128)(2,1)S(1)}, u32[]{:S(2)}, u32[]{:S(2)}) collective-permute-start(bf16[1,1,1,1,256,512]{5,4,3,2,1,0:T(8,128)(2,1)S(1)} %constant_dynamic-slice_fusion), channel_id=1, source_target_pairs={{0,2},{1,3},{2,0},{3,1},{4,6},{5,7},{6,4},{7,5},{8,10},{9,11},{10,... | collective-permute-start | bytes 786440 | tf_op jit(solution)/shard_map/ppermute | solution.py:296
  224.2 12.7 %copy-start.1 = (bf16[2048,512]{1,0:T(8,128)(2,1)S(1)}, bf16[2048,512]{1,0:T(8,128)(2,1)}, u32[]{:S(2)}) copy-start(bf16[2048,512]{1,0:T(8,128)(2,1)} %param.9) | copy-start | bytes 6291460
  (15 other events, 61.5 us)
